TPU v7x, 32 devices: a whole 2x2x4 slice. The times are simulated.
32 devices in a mesh: groups: 2 (over y), gx: 4 (over z), gy: 4 (over x, core).
Axes of the slice: x: 2, y: 2, z: 4, core: 2. Of those that a mesh axis runs over, the one named last changes fastest.
Arguments:
- tokens: bfloat16 [128, 16384], P(('groups', 'gy'), 'gx'), parts along dimension 0, may hold values from -6 to 6
- q_weight: bfloat16 [16384, 8192], P('gx', 'gy'), may hold values from -0.046875 to 0.046875
- k_weight: bfloat16 [16384, 512], P('gx', 'gy'), may hold values from -0.09375 to 0.09375
- v_weight: bfloat16 [16384, 512], P('gx', 'gy'), may hold values from -0.046875 to 0.046875
- out_weight: bfloat16 [8192, 16384], P('gy', 'gx'), may hold values from -0.0625 to 0.0625
- cache_keys: bfloat16 [16384, 512], P(('groups', 'gx'), 'gy'), parts along dimension 0, may hold values from -150 to 150
- cache_values: bfloat16 [16384, 512], P(('groups', 'gx'), 'gy'), parts along dimension 0, may hold values from -6 to 6
- tenant_ids: int32 [128], P('groups'), parts along dimension 0, may hold values from 0 to 7, never falling along the last dimension, each value on 1 to 16 neighbouring positions
- prefix_len: int32 [16], P('groups'), parts along dimension 0, may hold values from 1 to 8192, as said below
Outputs:
- mixed: bfloat16 [128, 16384], P(('groups', 'gy'), 'gx'), parts along dimension 0
There are 2 independent parts, one for each index of `groups`. A program takes and returns all parts, laid end to end along the dimension named above; an argument that names none is the same for every part. Nothing has to cross between parts.
Inputs may be any that keep to these rules, and one draw needn't show every extreme that they name: `prefix_len`: some tenant reads all 8192 positions.
All inputs are finite; a program needn't handle non-finite values.
Results may differ from a plain program's by a relative error of at most 0.012.
Values may be sent and summed in bfloat16 or wider, within the bound.
A program may use at most 128 MiB of HBM per device.

v0:
```python
import math

import jax
import jax.numpy as jnp
from jax import lax
from jax.sharding import PartitionSpec as P


def joined(part, axis, combine):
    gathered = jax.tree.map(lambda a: lax.all_gather(a, axis), part)

    def take(source):
        return jax.tree.map(lambda a: lax.dynamic_index_in_dim(a, source, 0, False), gathered)

    return lax.fori_loop(
        1, lax.axis_size(axis), lambda source, state: combine(state, take(source)), take(0)
    )


def combine_parts(left_part, right_part):
    left_peak, left_total, left_acc = left_part
    right_peak, right_total, right_acc = right_part
    joint_peak = jnp.maximum(left_peak, right_peak)
    left_factor = jnp.exp(left_peak - joint_peak)
    right_factor = jnp.exp(right_peak - joint_peak)
    joint_total = left_total * left_factor + right_total * right_factor
    joint_acc = left_acc * left_factor[..., None] + right_acc * right_factor[..., None]
    return (joint_peak, joint_total, joint_acc)


def body(
    tokens,
    q_weight,
    k_weight,
    v_weight,
    out_weight,
    cache_keys,
    cache_values,
    tenant_ids,
    prefix_len,
):
    head_dim = cache_keys.shape[1]
    q_width = q_weight.shape[1]
    head_group = q_width // head_dim
    total_tokens = tenant_ids.shape[0]
    own_rows = total_tokens // lax.axis_size("gx")
    gathered = lax.all_gather(tokens, "gy", axis=0, tiled=True)
    slab_rows = gathered
    projected = lax.psum_scatter(
        jnp.concatenate(
            [
                jnp.dot(slab_rows, q_weight, preferred_element_type=jnp.float32),
                jnp.dot(slab_rows, k_weight, preferred_element_type=jnp.float32),
                jnp.dot(slab_rows, v_weight, preferred_element_type=jnp.float32),
            ],
            axis=1,
        ),
        "gx",
        scatter_dimension=0,
        tiled=True,
    )
    own_queries = projected[:, :q_width].astype(jnp.bfloat16)
    new_keys = projected[:, q_width : q_width + head_dim].astype(jnp.bfloat16)
    new_values = projected[:, q_width + head_dim :].astype(jnp.bfloat16)
    queries = lax.all_gather(own_queries, "gx", axis=0, tiled=True)
    device_index = lax.axis_index("gx")
    tenant_count = prefix_len.shape[0]
    tenant_table = tenant_ids[:, None] == jnp.arange(tenant_count, dtype=jnp.int32)[None, :]
    prefix_of = jnp.sum(jnp.where(tenant_table, prefix_len[None, :], 0), axis=1)
    cache_rows = cache_keys.shape[0]
    key_pos = device_index * cache_rows + jnp.arange(cache_rows, dtype=jnp.int32)
    new_pos = device_index * own_rows + jnp.arange(own_rows, dtype=jnp.int32)
    new_tenant = lax.dynamic_slice_in_dim(tenant_ids, device_index * own_rows, own_rows, 0)
    block_tokens = math.gcd(total_tokens, max(1, 512 // head_group))
    score_scale = 1.0 / math.sqrt(head_dim)

    def attend_block(block_index):
        first_token = block_index * block_tokens
        q_rows = lax.dynamic_slice_in_dim(queries, first_token, block_tokens, 0).reshape(
            block_tokens * head_group, head_dim
        )
        rows_prefix = jnp.repeat(
            lax.dynamic_slice_in_dim(prefix_of, first_token, block_tokens, 0), head_group
        )
        rows_tenant = jnp.repeat(
            lax.dynamic_slice_in_dim(tenant_ids, first_token, block_tokens, 0), head_group
        )
        rows_pos = jnp.repeat(first_token + jnp.arange(block_tokens, dtype=jnp.int32), head_group)
        prefix_scores = (
            jnp.dot(q_rows, cache_keys.T, preferred_element_type=jnp.float32) * score_scale
        )
        allowed_prefix = key_pos[None, :] < rows_prefix[:, None]
        fresh_scores = jnp.dot(q_rows, new_keys.T, preferred_element_type=jnp.float32) * score_scale
        allowed_fresh = (new_tenant[None, :] == rows_tenant[:, None]) & (
            new_pos[None, :] <= rows_pos[:, None]
        )
        row_peak = jnp.maximum(
            jnp.max(jnp.where(allowed_prefix, prefix_scores, -1e30), axis=1),
            jnp.max(jnp.where(allowed_fresh, fresh_scores, -1e30), axis=1),
        )
        prefix_weights = jnp.where(
            allowed_prefix, jnp.exp(prefix_scores - row_peak[:, None]), 0.0
        ).astype(jnp.bfloat16)
        fresh_weights = jnp.where(
            allowed_fresh, jnp.exp(fresh_scores - row_peak[:, None]), 0.0
        ).astype(jnp.bfloat16)
        row_total = jnp.sum(prefix_weights.astype(jnp.float32), axis=1) + jnp.sum(
            fresh_weights.astype(jnp.float32), axis=1
        )
        row_acc = jnp.dot(prefix_weights, cache_values, preferred_element_type=jnp.float32)
        row_acc = row_acc + jnp.dot(fresh_weights, new_values, preferred_element_type=jnp.float32)
        return (
            row_peak.reshape(block_tokens, head_group),
            row_total.reshape(block_tokens, head_group),
            row_acc.reshape(block_tokens, head_group, head_dim),
        )

    peak_blocks, total_blocks, acc_blocks = lax.map(
        attend_block, jnp.arange(total_tokens // block_tokens, dtype=jnp.int32)
    )
    row_peaks = peak_blocks.reshape(total_tokens, head_group)
    row_totals = total_blocks.reshape(total_tokens, head_group)
    row_accs = acc_blocks.reshape(total_tokens, head_group, head_dim)
    joint_peak, joint_total, joint_acc = joined(
        (row_peaks, row_totals, row_accs), "gx", combine_parts
    )
    attended = (
        (joint_acc / joint_total[..., None]).astype(jnp.bfloat16).reshape(total_tokens, q_width)
    )
    slab_rows = attended
    mixed = lax.psum_scatter(
        jnp.dot(slab_rows, out_weight, preferred_element_type=jnp.float32),
        "gy",
        scatter_dimension=0,
        tiled=True,
    )
    return mixed.astype(jnp.bfloat16)


def solution(mesh):
    placed = (
        P(("groups", "gy"), "gx"),
        P("gx", "gy"),
        P("gx", "gy"),
        P("gx", "gy"),
        P("gy", "gx"),
        P(("groups", "gx"), "gy"),
        P(("groups", "gx"), "gy"),
        P("groups"),
        P("groups"),
    )
    return jax.shard_map(
        body, mesh=mesh, in_specs=placed, out_specs=P(("groups", "gy"), "gx"), check_vma=False
    )
```

profile of v0, /device:TPU:0, one launch (start us, length us, event | category | flops | bytes accessed | tf_op | source)
XLA Modules:
  0.0 169.6 jit_solution(5925290121575181558)
XLA Ops:
  6.5 8.9 %all_gather.15 = bf16[64,4096]{1,0:T(8,128)(2,1)S(1)} all-gather(bf16[16,4096]{1,0:T(8,128)(2,1)} %param.13), channel_id=1, replica_groups=mesh['groups'=2,'gx'=4,'gy'=4] {'gy'}, dimensions={0}, use_global_device_ids=true | all-gather | bytes 655360 | tf_op jit(solution)/shard_map/all_gather | solution.py:47
  15.5 8.9 %fusion.16 = f32[64,2048]{1,0:T(8,128)S(1)} fusion(bf16[64,4096]{1,0:T(8,128)(2,1)S(1)} %all_gather.15, bf16[4096,2048]{1,0:T(8,128)(2,1)} %param.14), kind=kOutput, calls=%fused_computation.40 | convolution fusion | flops 1073741824 | bytes 17825792 | tf_op jit(solution)/shard_map/dot_general | solution.py:52
  24.4 0.3 fusion.17
  24.8 0.3 fusion.18
  25.1 0.9 pad_maximum_fusion
  26.1 0.1 dynamic_slice.57
  26.2 0.1 select_reduce_fusion.1
  26.3 22.7 %reduce-scatter.3.cloned.1.call-done = f32[16,2304]{1,0:T(8,128)} async-done(((f32[64,2304]{1,0:T(8,128)}), f32[16,2304]{1,0:T(8,128)}) %reduce-scatter.3.cloned.1.call-update) | async-done | bytes 147472 | tf_op jit(solution)/shard_map/reduce_scatter | solution.py:49
  49.0 0.9 convert.5
  49.9 14.3 %all_gather.16 = bf16[64,2048]{1,0:T(8,128)(2,1)S(1)} all-gather(bf16[16,2048]{1,0:T(8,128)(2,1)S(1)} %slice.18), channel_id=1, replica_groups=mesh['groups'=2,'gx'=4,'gy'=4] {'gx'}, dimensions={0}, use_global_device_ids=true | all-gather | bytes 327680 | tf_op jit(solution)/shard_map/all_gather | solution.py:65
  64.3 11.0 %while.35 = (s32[]{:T(128)}, f32[2,32,16]{2,1,0:T(8,128)S(1)}, f32[2,32,16]{2,1,0:T(8,128)S(1)}, f32[2,32,16,128]{3,2,1,0:T(8,128)S(1)}, s32[2]{0:T(128)S(1)}, /...) while((s32[]{:T(128)}, f32[2,32,16]{2,1,0:T(8,128)S(1)}, ...), condition=%wide.region_7.8_spmd.clone, body=%wide.region_2.7_spmd.clone.sunk | while | flops 552780864 | bytes 15990343 | solution.py:118
  64.3 0.6 dynamic_slice.87
  65.6 0.1 dynamic_slice.89
  65.7 0.1 broadcast_in_dim.88
  65.7 0.1 eq.61
  65.8 0.1 broadcast_in_dim.87
  65.9 0.1 le.38
  66.0 0.2 select_reduce_fusion.3
  66.2 0.1 dynamic_slice.88
  66.3 0.1 broadcast_in_dim.86
  66.3 0.1 lt.83
  66.4 0.9 fusion.56
  67.3 1.2 convert_reduce_fusion.4
  68.5 0.1 convert_reduce_fusion.5
  68.6 0.2 fusion.57
  68.8 0.7 convolution_add_fusion.2
  69.6 0.1 add.175
  69.7 0.1 max.34
  69.8 0.6 dynamic_slice.87
  71.1 0.1 dynamic_slice.89
  71.2 0.1 broadcast_in_dim.88
  71.2 0.1 eq.61
  71.4 0.1 le.38
  71.5 0.2 select_reduce_fusion.3
  71.7 0.1 dynamic_slice.88
  71.7 0.1 broadcast_in_dim.86
  71.8 0.1 lt.83
  71.9 0.9 fusion.56
  72.8 1.2 convert_reduce_fusion.4
  74.0 0.1 convert_reduce_fusion.5
  74.1 0.2 fusion.57
  74.3 0.7 convolution_add_fusion.2
  75.1 0.1 add.175
  75.2 0.1 max.34
  75.3 0.8 copy-done.3
  76.2 13.3 %all_gather.18 = f32[4,64,16]{1,2,0:T(8,128)S(1)} all-gather(f32[1,64,16]{1,2,0:T(8,128)S(1)} %copy.29), channel_id=1, replica_groups=mesh['groups'=2,'gx'=4,'gy'=4] {'gx'}, dimensions={0}, use_global_device_ids=true | all-gather | bytes 20480 | tf_op jit(solution)/shard_map/all_gather | solution.py:10
  89.6 13.5 %all_gather.17 = f32[4,64,16]{1,2,0:T(8,128)S(1)} all-gather(f32[1,64,16]{1,2,0:T(8,128)S(1)} %copy.28), channel_id=1, replica_groups=mesh['groups'=2,'gx'=4,'gy'=4] {'gx'}, dimensions={0}, use_global_device_ids=true | all-gather | bytes 20480 | tf_op jit(solution)/shard_map/all_gather | solution.py:10
  103.0 18.4 %all-gather.2.cloned.1.call-done = f32[4,64,16,128]{3,2,1,0:T(8,128)} async-done(((f32[1,64,16,128]{3,2,1,0:T(8,128)}), f32[4,64,16,128]{3,2,1,0:T(8,128)}) %all-gather.2.cloned.1.call-update) | async-done | bytes 2097168 | tf_op jit(solution)/shard_map/all_gather | solution.py:10
  121.4 1.1 slice_bitcast_fusion
  122.5 5.0 %while.34 = (s32[]{:T(128)}, f32[64,16]{0,1:T(8,128)S(1)}, f32[64,16]{0,1:T(8,128)S(1)}, f32[64,16,128]{2,1,0:T(8,128)S(1)}, f32[4,64,16]{1,2,0:T(8,128)S(1)}, /...) while((s32[]{:T(128)}, f32[64,16]{0,1:T(8,128)S(1)}, ...), condition=%wide.region_9.10_spmd, body=%wide.region_8.9_spmd.sunk | while | flops 399365 | bytes 1630359 | solution.py:15
  122.5 0.1 copy.37
  122.6 0.1 copy.38
  122.7 1.4 fusion.47
  124.2 0.1 copy.37
  124.3 0.1 copy.38
  124.4 1.4 fusion.47
  125.8 0.1 copy.37
  125.9 0.1 copy.38
  126.0 1.4 fusion.47
  127.5 0.1 copy.27
  127.5 0.2 divide_convert_fusion
  127.8 9.8 %fusion.9 = f32[64,4096]{1,0:T(8,128)} fusion(bf16[2048,4096]{1,0:T(8,128)(2,1)} %param.17, bf16[8,8,16,128]{3,2,1,0:T(8,128)(2,1)S(1)} %bitcast.70), kind=kOutput, calls=%fused_computation.31 | convolution fusion | flops 1073741824 | bytes 18087936 | tf_op jit(solution)/shard_map/dot_general | solution.py:132
  137.5 23.9 %reduce-scatter.5.cloned.1.call-done = f32[16,4096]{1,0:T(8,128)} async-done(((f32[64,4096]{1,0:T(8,128)}), f32[16,4096]{1,0:T(8,128)}) %reduce-scatter.5.cloned.1.call-update) | async-done | bytes 262160 | tf_op jit(solution)/shard_map/reduce_scatter | solution.py:131
  161.5 1.6 convert_element_type.22
  (51 shorter events, 0.7 us)
Async XLA Ops:
  6.5 17.9 %copy-start = (bf16[4096,128]{1,0:T(8,128)(2,1)S(1)}, bf16[4096,128]{1,0:T(8,128)(2,1)}, u32[]{:S(2)}) copy-start(bf16[4096,128]{1,0:T(8,128)(2,1)} %param.15) | copy-start | bytes 3145732
  6.5 42.4 %reduce-scatter.3.cloned.1.call-start = ((), (), s32[]{:S(2)}) async-start(), calls=%async_computation.2 | async-start | bytes 737280 | tf_op jit(solution)/shard_map/reduce_scatter | solution.py:49
  15.5 9.3 %copy-start.2 = (bf16[4096,128]{1,0:T(8,128)(2,1)S(1)}, bf16[4096,128]{1,0:T(8,128)(2,1)}, u32[]{:S(2)}) copy-start(bf16[4096,128]{1,0:T(8,128)(2,1)} %param.16) | copy-start | bytes 3145732
  24.4 1.7 copy-start.6
  24.4 1.8 %copy-start.5 = (s32[8]{0:T(128)S(1)}, s32[8]{0:T(128)}, u32[]{:S(2)}) copy-start(s32[8]{0:T(128)} %param.21) | copy-start | bytes 100
  24.4 39.8 %copy-start.1 = (bf16[2048,128]{1,0:T(8,128)(2,1)S(1)}, bf16[2048,128]{1,0:T(8,128)(2,1)}, u32[]{:S(2)}) copy-start(bf16[2048,128]{1,0:T(8,128)(2,1)} %param.19) | copy-start | bytes 1572868
  24.4 39.8 %copy-start.4 = (bf16[2048,128]{1,0:T(8,128)(2,1)S(1)}, bf16[2048,128]{1,0:T(8,128)(2,1)}, u32[]{:S(2)}) copy-start(bf16[2048,128]{1,0:T(8,128)(2,1)} %param.18) | copy-start | bytes 1572868
  26.0 95.4 %all-gather.2.cloned.1.call-start = ((), (), s32[]{:S(2)}) async-start(), calls=%async_computation.3 | async-start | bytes 2621440 | tf_op jit(solution)/shard_map/all_gather | solution.py:10
  75.2 0.8 copy-start.3
  76.1 85.4 %reduce-scatter.5.cloned.1.call-start = ((), (), s32[]{:S(2)}) async-start(), calls=%async_computation.4 | async-start | bytes 1310720 | tf_op jit(solution)/shard_map/reduce_scatter | solution.py:131
Sparse Core Ops, SparseCore 0:
  26.1 22.7 reduce-scatter.2
  76.2 45.1 all-gather.1
  137.7 23.7 reduce-scatter.4
where the time goes:
time: 170 us
  waiting for transfers between devices  65 us (38%)
  blocking collectives  50.1 us (29%)
  matrix products  23.3 us (14%)
  between operations  13.3 us (8%)
  other arithmetic  10.7 us (6%)
  local copies, waits for them, and re-layouts  5.66 us (3%)
    all_gather x2, blocking collectives, joined(): gathered = jax.tree.map(lambda a: lax.all_gather(a, axis), part)  26.8 us
    reduce_scatter x1, waiting for transfers between devices, body(): lax.psum_scatter(jnp.dot(slab_rows, out_weight, preferred_element_type=jn...  23.9 us
    reduce_scatter x1, waiting for transfers between devices, body(): lax.psum_scatter(jnp.concatenate([jnp.dot(slab_rows, q_weight, preferred_...  22.7 us
    all_gather x1, waiting for transfers between devices, joined(): gathered = jax.tree.map(lambda a: lax.all_gather(a, axis), part)  18.4 us
    all_gather x1, blocking collectives, body(): queries = lax.all_gather(own_queries, 'gx', axis=0, tiled=True)  14.3 us
    dot_general x1, matrix products, body(): jnp.dot(slab_rows, out_weight, preferred_element_type=jnp.float32)  9.76 us
    all_gather x1, blocking collectives, body(): gathered = lax.all_gather(tokens, 'gy', axis=0, tiled=True)  8.95 us
    dot_general x1, matrix products, body(): jnp.dot(slab_rows, q_weight, preferred_element_type=jnp.float32)  8.89 us
  transfers between devices with their start and end apart: 3, of which 3 were waited for; matrix products, arithmetic and copies ran while one was open for 0% of the time, Pallas kernels for 0%

commit v1 on v0

--- a/solution.py
+++ b/solution.py
@@ -1,9 +1,540 @@
+import functools
 import math
 
 import jax
 import jax.numpy as jnp
 from jax import lax
+from jax.experimental import pallas as pl
+from jax.experimental.pallas import tpu as pltpu
 from jax.sharding import PartitionSpec as P
+
+BF = jnp.bfloat16
+F32 = jnp.float32
+WIRE = jnp.float32
+TILE = 256
+ROWS = 16
+
+
+def fused(
+    nx,
+    ny,
+    heads,
+    hd,
+    hpg,
+    tokens,
+    q_weight,
+    k_weight,
+    v_weight,
+    out_weight,
+    cache_keys,
+    cache_values,
+    tenants,
+    prefix_len,
+    out,
+    tok_full,
+    wq,
+    wkv,
+    wo,
+    kbuf,
+    vbuf,
+    vones,
+    bias,
+    part,
+    wire,
+    recv_end,
+    recv_mid,
+    fresh,
+    q_full,
+    scores,
+    o_part,
+    l_part,
+    o_wire,
+    l_wire,
+    o_end,
+    l_end,
+    o_mid,
+    l_mid,
+    att_full,
+    macc,
+    o2_send,
+    recv3,
+    pair_sum,
+    recv4,
+    load_sem,
+    tok_sem,
+    up_sem,
+    across_sem,
+    down_sem,
+    o_up_sem,
+    o_across_sem,
+    l_up_sem,
+    l_across_sem,
+    o_down_sem,
+    r3_sem,
+    r4_sem,
+):
+    ix = lax.axis_index("gx")
+    iy = lax.axis_index("gy")
+    width = heads * hd
+    groups = heads // hpg
+    gw = hpg * hd
+    total = nx * ROWS
+    cache_rows = cache_keys.shape[0]
+    scale = math.log2(math.e) / math.sqrt(hd)
+
+    def load(src, dst, i):
+        copy = pltpu.make_async_copy(src, dst, load_sem.at[i])
+        copy.start()
+        return copy
+
+    end = (ix == 0) | (ix == nx - 1)
+    mid = jnp.logical_not(end)
+    inner = jnp.where(ix == 0, 1, nx - 2)
+    outer = jnp.where(ix == 1, 0, nx - 1)
+    other = nx - 1 - ix
+    core = lax.rem(iy, 2)
+    cell = iy // 2
+    sibling = iy + 1 - 2 * core
+    across = lax.rem(iy + 2, ny)
+
+    def remote(src, dst, sems, axis, target):
+        return pltpu.make_async_remote_copy(
+            src_ref=src,
+            dst_ref=dst,
+            send_sem=sems.at[0],
+            recv_sem=sems.at[1],
+            device_id={axis: target},
+            device_id_type=pl.DeviceIdType.MESH,
+        )
+
+    def signal(axis, target):
+        pl.semaphore_signal(
+            barrier, inc=1, device_id={axis: target}, device_id_type=pl.DeviceIdType.MESH
+        )
+
+    own_tokens = load(tokens, tok_full.at[iy], 0)
+    wk_copy = load(k_weight, wkv.at[:, :hd], 1)
+    wv_copy = load(v_weight, wkv.at[:, hd:], 2)
+    wq_copies = [
+        load(q_weight.at[:, pl.ds(c * gw, gw)], wq.at[:, pl.ds(c * gw, gw)], 3 + c)
+        for c in range(groups)
+    ]
+    key_copy = load(cache_keys, kbuf.at[pl.ds(0, cache_rows)], 3 + groups)
+    value_copy = load(cache_values, vbuf.at[pl.ds(0, cache_rows)], 4 + groups)
+
+    barrier = pltpu.get_barrier_semaphore()
+    signal("gy", sibling)
+    signal("gy", across)
+
+    @pl.when(end)
+    def _():
+        signal("gx", inner)
+        pl.semaphore_wait(barrier, 3)
+
+    @pl.when(mid)
+    def _():
+        signal("gx", outer)
+        signal("gx", other)
+        pl.semaphore_wait(barrier, 4)
+
+    tok_across = remote(tokens, tok_full.at[iy], tok_sem.at[0], "gy", across)
+    tok_across.start()
+    tok_pair = remote(tokens, tok_full.at[iy], tok_sem.at[1], "gy", sibling)
+    tok_pair.start()
+
+    tid_row = tenants[...].astype(F32)
+    r = lax.broadcasted_iota(jnp.int32, (total, total), 0)
+    l = lax.broadcasted_iota(jnp.int32, (total, total), 1)
+    tid = jnp.sum(
+        jnp.where(r == l, jnp.broadcast_to(tid_row, (total, total)), 0.0), axis=1, keepdims=True
+    )
+    reach = jnp.zeros((total, 1), jnp.int32)
+    for i in range(prefix_len.shape[0]):
+        reach = jnp.where(tid == float(i), prefix_len[i], reach)
+    pos = lax.broadcasted_iota(jnp.int32, (total, cache_rows), 1) + ix * cache_rows
+    bias[:, pl.ds(0, cache_rows)] = jnp.where(pos < reach, 0.0, -1e30)
+    row = lax.broadcasted_iota(jnp.int32, (total, 128), 0)
+    lane = lax.broadcasted_iota(jnp.int32, (total, 128), 1)
+    half = total // 2
+    new = lane + (ix - 1) * half
+    new_tid = jnp.sum(jnp.where(row == new, tid, 0.0), axis=0, keepdims=True)
+    ok = (new_tid == tid) & (new <= row) & (lane < half) & (new >= 0)
+    bias[:, pl.ds(cache_rows, 128)] = jnp.where(ok, 0.0, -1e30)
+    vones[...] = jnp.ones_like(vones)
+    kbuf[pl.ds(cache_rows, 128), :] = jnp.zeros((128, hd), BF)
+    vbuf[pl.ds(cache_rows, 128), :] = jnp.zeros((128, hd), BF)
+
+    wo_copies = []
+    eye = row == lane
+    level = lax.broadcasted_iota(jnp.int32, (8, 128), 0)
+
+    def to_lanes(columns):
+        tile = jnp.zeros((8, 128), F32)
+        for h, column in enumerate(columns):
+            flat = jnp.sum(jnp.where(eye, column, 0.0), axis=0, keepdims=True)
+            tile = jnp.where(level == h, flat, tile)
+        return tile
+
+    def from_lanes(tile, h):
+        return jnp.sum(jnp.where(eye, tile[h : h + 1, :], 0.0), axis=1, keepdims=True)
+
+    def span_of(c):
+        return pl.ds(c * gw, gw if c < groups else 2 * hd)
+
+    def up(c):
+        return remote(wire.at[:, span_of(c)], recv_end.at[:, span_of(c)], up_sem.at[c], "gx", inner)
+
+    def over(c):
+        return remote(wire.at[:, span_of(c)], recv_mid.at[:, span_of(c)], across_sem.at[c], "gx", other)
+
+    def down(c):
+        return remote(q_full.at[:, span_of(c)], q_full.at[:, span_of(c)], down_sem.at[c], "gx", outer)
+
+    def o_up(c):
+        return (
+            remote(l_wire.at[c], l_end.at[c], l_up_sem.at[c], "gx", inner),
+            remote(o_wire.at[c], o_end.at[c], o_up_sem.at[c], "gx", inner),
+        )
+
+    def o_over(c):
+        return (
+            remote(l_wire.at[c], l_mid.at[c], l_across_sem.at[c], "gx", other),
+            remote(o_wire.at[c], o_mid.at[c], o_across_sem.at[c], "gx", other),
+        )
+
+    def o_down(c):
+        return remote(
+            att_full.at[:, span_of(c)], att_full.at[:, span_of(c)], o_down_sem.at[c], "gx", outer
+        )
+
+    def project(c):
+        base = c * gw
+        span = gw if c < groups else 2 * hd
+        if c < groups:
+            wq_copies[c].wait()
+            wo_copies.append(
+                load(out_weight.at[pl.ds(base, gw)], wo.at[pl.ds(base, gw)], 5 + groups + c)
+            )
+        else:
+            wk_copy.wait()
+            wv_copy.wait()
+
+        @pl.loop(0, span // TILE)
+        def _(i):
+            at = pl.multiple_of(i * TILE, TILE)
+            w = wq[:, pl.ds(base + at, TILE)] if c < groups else wkv[:, pl.ds(at, TILE)]
+            y = jnp.dot(
+                tok_full[...].reshape(total, -1), w, preferred_element_type=F32
+            )
+            part[:, pl.ds(base + at, TILE)] = y
+
+            @pl.when(end)
+            def _():
+                wire[:, pl.ds(base + at, TILE)] = y.astype(WIRE)
+
+        @pl.when(end)
+        def _():
+            up(c).start()
+
+    def pass_on(c):
+        @pl.when(mid)
+        def _():
+            up(c).wait_recv()
+            cols = span_of(c)
+            y = part[:, cols] + recv_end[:, cols].astype(F32)
+            part[:, cols] = y
+            wire[:, cols] = y.astype(WIRE)
+            over(c).start()
+
+    def settle(c):
+        if c == groups:
+            key_copy.wait()
+            value_copy.wait()
+
+        @pl.when(mid)
+        def _():
+            over(c).wait_recv()
+            cols = span_of(c)
+            y = (part[:, cols] + recv_mid[:, cols].astype(F32)).astype(BF)
+            if c == groups:
+                fresh[...] = y.reshape(2, half, 2 * hd)
+                own = fresh[ix - 1]
+                kbuf[pl.ds(cache_rows, half), :] = own[:, :hd]
+                vbuf[pl.ds(cache_rows, half), :] = own[:, hd:]
+            else:
+                q_full[:, cols] = y
+                down(c).start()
+
+    tiles = [(a, min(512, cache_rows - a)) for a in range(0, cache_rows, 512)]
+    tiles.append((cache_rows, 128))
+
+    def attend(c):
+        @pl.when(end)
+        def _():
+            down(c).wait_recv()
+
+        q = jnp.concatenate(
+            [
+                q_full[:, pl.ds(c * gw + h * hd, hd)]
+                for h in range(hpg)
+            ],
+            axis=0,
+        )
+        peak = jnp.full((hpg * total, 1), -1e20, F32)
+        for a, t in tiles:
+            s = lax.dot_general(
+                q,
+                kbuf[pl.ds(a, t), :],
+                (((1,), (1,)), ((), ())),
+                preferred_element_type=F32,
+            )
+            s = (s * scale).reshape(hpg, total, t) + bias[:, pl.ds(a, t)][None]
+            s = s.reshape(hpg * total, t)
+            scores[:, pl.ds(a, t)] = s
+            peak = jnp.maximum(peak, jnp.max(s, axis=1, keepdims=True))
+        acc = jnp.zeros((hpg * total, 2 * hd), F32)
+        for a, t in tiles:
+            p = jnp.exp2(scores[:, pl.ds(a, t)] - peak).astype(BF)
+            v = jnp.concatenate([vbuf[pl.ds(a, t), :], vones[pl.ds(0, t), :]], axis=1)
+            acc = acc + jnp.dot(p, v, preferred_element_type=F32)
+        norm = acc[:, hd : hd + 1]
+        some = norm > 0.0
+        o = acc[:, :hd] / jnp.where(some, norm, 1.0)
+        lse = jnp.where(some, peak + jnp.log2(jnp.where(some, norm, 1.0)), -1e20)
+        parts = [slice(h * total, (h + 1) * total) for h in range(hpg)]
+        tile = to_lanes([lse[rows] for rows in parts])
+        wide = jnp.concatenate([o[rows] for rows in parts], axis=1)
+
+        @pl.when(end)
+        def _():
+            l_wire[c] = tile
+            o_wire[c] = wide.astype(BF)
+            for copy in o_up(c):
+                copy.start()
+
+        @pl.when(mid)
+        def _():
+            l_part[c] = tile
+            o_part[c] = wide
+
+    def merged(c, o_ref, l_ref):
+        mine, theirs = l_part[c], l_ref[c]
+        top = jnp.maximum(mine, theirs)
+        left, right = jnp.exp2(mine - top), jnp.exp2(theirs - top)
+        both = left + right
+        left, right = left / both, right / both
+        pieces = []
+        for h in range(hpg):
+            cols = pl.ds(h * hd, hd)
+            pieces.append(
+                o_part[c, :, cols] * from_lanes(left, h)
+                + o_ref[c, :, cols].astype(F32) * from_lanes(right, h)
+            )
+        return jnp.concatenate(pieces, axis=1), top + jnp.log2(both)
+
+    def merge(c):
+        @pl.when(mid)
+        def _():
+            for copy in o_up(c):
+                copy.wait_recv()
+            wide, tile = merged(c, o_end, l_end)
+            l_part[c] = tile
+            o_part[c] = wide
+            l_wire[c] = tile
+            o_wire[c] = wide.astype(BF)
+            for copy in o_over(c):
+                copy.start()
+
+    def finish(c):
+        @pl.when(mid)
+        def _():
+            for copy in o_over(c):
+                copy.wait_recv()
+            wide, _ = merged(c, o_mid, l_mid)
+            att_full[:, span_of(c)] = wide.astype(BF)
+            o_down(c).start()
+
+    out_cols = out.shape[1]
+    spans = 4
+    sw = out_cols // spans
+
+    def pair_copy(n):
+        cols = pl.ds(n * sw, sw)
+        return remote(
+            o2_send.at[:, 1 - core, :, cols], recv3.at[:, :, cols], r3_sem.at[n], "gy", sibling
+        )
+
+    def cell_copy(n):
+        cols = pl.ds(n * sw, sw)
+        return remote(pair_sum.at[:, cols], recv4.at[:, cols], r4_sem.at[n], "gy", across)
+
+    def pair(n):
+        cols = pl.ds(n * sw, sw)
+        pair_copy(n).wait_recv()
+        y = o2_send[1 - cell, core, :, cols].astype(F32) + recv3[1 - cell, :, cols].astype(F32)
+        pair_sum[:, cols] = y.astype(BF)
+        cell_copy(n).start()
+
+
+    def mix(c):
+        @pl.when(end)
+        def _():
+            o_down(c).wait_recv()
+
+        wo_copies[c].wait()
+        last = c == groups - 1
+
+        def columns(at):
+            a = att_full[:, pl.ds(c * gw, gw)]
+            y = jnp.dot(
+                a, wo[pl.ds(c * gw, gw), pl.ds(at, TILE)], preferred_element_type=F32
+            )
+            if c > 0:
+                y = y + macc[:, pl.ds(at, TILE)]
+            if last:
+                o2_send[:, :, :, pl.ds(at, TILE)] = y.astype(BF).reshape(2, 2, ROWS, TILE)
+            else:
+                macc[:, pl.ds(at, TILE)] = y
+
+        if not last:
+
+            @pl.loop(0, out_cols // TILE)
+            def _(i):
+                columns(pl.multiple_of(i * TILE, TILE))
+
+            return
+        for n in range(spans):
+
+            @pl.loop(0, sw // TILE)
+            def _(i):
+                columns(pl.multiple_of(n * sw + i * TILE, TILE))
+
+            pair_copy(n).start()
+            if n > 0:
+                pair(n - 1)
+        pair(spans - 1)
+
+    own_tokens.wait()
+    tok_across.wait_recv()
+    tok_relay = remote(tok_full.at[across], tok_full.at[across], tok_sem.at[2], "gy", sibling)
+    tok_relay.start()
+    tok_pair.wait_recv()
+    tok_relay.wait_recv()
+    steps = ('Pk', 'P0', 'P1', 'Xk', 'P2', 'X0', 'P3', 'X1', 'Yk', 'Y0', 'X2', 'Y1', 'X3', 'A0', 'Y2', 'A1', 'Y3', 'A2', 'A3', 'U0', 'U1', 'V0', 'U2', 'V1', 'M0', 'U3', 'V2', 'M1', 'V3', 'M2', 'M3')
+    table = dict(P=project, X=pass_on, Y=settle, A=attend, U=merge, V=finish, M=mix)
+    for step in steps:
+        table[step[0]](groups if step[1] == "k" else int(step[1]))
+
+    for n in range(spans):
+        cols = pl.ds(n * sw, sw)
+        y = o2_send[cell, core, :, cols].astype(F32) + recv3[cell, :, cols].astype(F32)
+        cell_copy(n).wait_recv()
+        out[:, cols] = (y + recv4[:, cols].astype(F32)).astype(BF)
+
+    tok_across.wait_send()
+    tok_pair.wait_send()
+    tok_relay.wait_send()
+    for n in range(spans):
+        pair_copy(n).wait_send()
+        cell_copy(n).wait_send()
+
+    @pl.when(end)
+    def _():
+        for c in range(groups + 1):
+            up(c).wait_send()
+        for c in range(groups):
+            for copy in o_up(c):
+                copy.wait_send()
+
+    @pl.when(mid)
+    def _():
+        for c in range(groups + 1):
+            over(c).wait_send()
+        for c in range(groups):
+            down(c).wait_send()
+            o_down(c).wait_send()
+            for copy in o_over(c):
+                copy.wait_send()
+
+
+def fused_body(nx, ny, *args):
+    tokens, q_weight, k_weight, v_weight, out_weight, cache_keys, cache_values, tenant_ids, prefix_len = args
+    hd = cache_keys.shape[1]
+    width = q_weight.shape[1]
+    heads = width // hd
+    groups = 4
+    hpg = heads // groups
+    gw = hpg * hd
+    total = tenant_ids.shape[0]
+    depth = tokens.shape[1]
+    out_cols = out_weight.shape[1]
+    rows = cache_keys.shape[0] + 128
+    anywhere = pl.BlockSpec(memory_space=pl.ANY)
+    vmem = pl.BlockSpec(memory_space=pltpu.VMEM)
+    dma = pltpu.SemaphoreType.DMA
+    chunks = groups + 1
+    return pl.pallas_call(
+        functools.partial(fused, nx, ny, heads, hd, hpg),
+        out_shape=jax.ShapeDtypeStruct((ROWS, out_cols), BF),
+        in_specs=[anywhere] * 7 + [vmem, pl.BlockSpec(memory_space=pltpu.SMEM)],
+        out_specs=vmem,
+        scratch_shapes=[
+            pltpu.VMEM((ny, ROWS, depth), BF),
+            pltpu.VMEM((depth, width), BF),
+            pltpu.VMEM((depth, 2 * hd), BF),
+            pltpu.VMEM((width, out_cols), BF),
+            pltpu.VMEM((rows, hd), BF),
+            pltpu.VMEM((rows, hd), BF),
+            pltpu.VMEM((512, hd), BF),
+            pltpu.VMEM((total, rows), F32),
+            pltpu.VMEM((total, width + 2 * hd), F32),
+            pltpu.VMEM((total, width + 2 * hd), WIRE),
+            pltpu.VMEM((total, width + 2 * hd), WIRE),
+            pltpu.VMEM((total, width + 2 * hd), WIRE),
+            pltpu.VMEM((2, total // 2, 2 * hd), BF),
+            pltpu.VMEM((total, width), BF),
+            pltpu.VMEM((hpg * total, rows), F32),
+            pltpu.VMEM((groups, total, gw), F32),
+            pltpu.VMEM((groups, 8, 128), F32),
+            pltpu.VMEM((groups, total, gw), BF),
+            pltpu.VMEM((groups, 8, 128), F32),
+            pltpu.VMEM((groups, total, gw), BF),
+            pltpu.VMEM((groups, 8, 128), F32),
+            pltpu.VMEM((groups, total, gw), BF),
+            pltpu.VMEM((groups, 8, 128), F32),
+            pltpu.VMEM((total, width), BF),
+            pltpu.VMEM((total, out_cols), F32),
+            pltpu.VMEM((2, 2, ROWS, out_cols), BF),
+            pltpu.VMEM((2, ROWS, out_cols), BF),
+            pltpu.VMEM((ROWS, out_cols), BF),
+            pltpu.VMEM((ROWS, out_cols), BF),
+            dma((5 + 2 * groups,)),
+            dma((3, 2)),
+            dma((chunks, 2)),
+            dma((chunks, 2)),
+            dma((groups, 2)),
+            dma((groups, 2)),
+            dma((groups, 2)),
+            dma((groups, 2)),
+            dma((groups, 2)),
+            dma((groups, 2)),
+            dma((4, 2)),
+            dma((4, 2)),
+        ],
+        compiler_params=pltpu.CompilerParams(
+            collective_id=0, has_side_effects=True, vmem_limit_bytes=56 * 2**20
+        ),
+    )(
+        tokens,
+        q_weight,
+        k_weight,
+        v_weight,
+        out_weight,
+        cache_keys,
+        cache_values,
+        tenant_ids.reshape(1, total),
+        prefix_len,
+    )
 
 
 def joined(part, axis, combine):
@@ -149,6 +680,14 @@
         P("groups"),
         P("groups"),
     )
+    nx, ny = mesh.shape["gx"], mesh.shape["gy"]
+
+    def local(*args):
+        whole = args[7].shape[0]
+        if nx == ny == 4 and whole == nx * ROWS:
+            return fused_body(nx, ny, *args)
+        return body(*args)
+
     return jax.shard_map(
-        body, mesh=mesh, in_specs=placed, out_specs=P(("groups", "gy"), "gx"), check_vma=False
-    )
+        local, mesh=mesh, in_specs=placed, out_specs=P(("groups", "gy"), "gx"), check_vma=False
+    )

time: 170 us -> 59.8 us (0.35)
  waiting for transfers between devices: 65 us -> 0 us
  Pallas kernels: 0 us -> 58.1 us
  blocking collectives: 50.1 us -> 0 us
  matrix products: 23.3 us -> 0 us
  between operations: 13.3 us -> 0.01 us
  other arithmetic: 10.7 us -> 0 us
  local copies, waits for them, and re-layouts: 5.66 us -> 1.57 us
    pallas_call x0 -> x1, Pallas kernels: none -> 58.1 us  [fused_body(): pl.pallas_call(functools.partial(fused, nx, ny, heads, hd, hpg), out_shap...]
    all_gather x4 -> x0, blocking collectives: 50.1 us -> none  [the longest x2 26.8 us: joined(): gathered = jax.tree.map(lambda a: lax.all_gather(a, axis), part)]
    reduce_scatter x2 -> x0, waiting for transfers between devices: 46.6 us -> none  [the longest x1 23.9 us: body(): lax.psum_scatter(jnp.dot(slab_rows, out_weight, preferred_element_type=jn...]
    dot_general x12 -> x0, matrix products: 23.3 us -> none  [the longest x1 9.76 us: body(): jnp.dot(slab_rows, out_weight, preferred_element_type=jnp.float32)]
    all_gather x1 -> x0, waiting for transfers between devices: 18.4 us -> none  [joined(): gathered = jax.tree.map(lambda a: lax.all_gather(a, axis), part)]
    add x14 -> x0, other arithmetic: 4.4 us -> none  [the longest x3 4.31 us: combine_parts(): left_acc * left_factor[..., None] + right_acc * right_factor[..., None]]
    reduce_sum x5 -> x0, other arithmetic: 2.63 us -> none  [the longest x2 2.37 us: attend_block(): jnp.sum(prefix_weights.astype(jnp.float32), axis=1)]
    convert_element_type x2 -> x0, other arithmetic: 1.83 us -> none  [the longest x1 1.62 us: body(): return mixed.astype(jnp.bfloat16)]
  transfers between devices with their start and end apart: 3 -> 0, of which waited for: 3 -> 0; matrix products, arithmetic and copies ran while one was open for 0% -> 0% of each run, Pallas kernels for 0% -> 0%
where the time goes in v1:
time: 59.8 us; the launch traced here: 59.7 us
  Pallas kernels  58.1 us (97%)
  local copies, waits for them, and re-layouts  1.57 us (3%)
    pallas_call x1, Pallas kernels, fused_body(): pl.pallas_call(functools.partial(fused, nx, ny, heads, hd, hpg), out_shap...  58.1 us
    unnamed x1, local copies, waits for them, and re-layouts  1.57 us

profile of v1, /device:TPU:0, one launch (start us, length us, event | category | flops | bytes accessed | tf_op | source)
XLA Modules:
  0.0 59.7 jit_solution(4536911154147001870)
XLA Ops:
  0.0 58.1 %shard_map.91 = bf16[16,4096]{1,0:T(8,128)(2,1)} custom-call(bf16[16,4096]{1,0:T(8,128)(2,1)} %tokens.1, bf16[4096,2048]{1,0:T(8,128)(2,1)} %q_weight.1, bf16[4096,128]{1,0:T(8,128)(2,1)} %k_weight.1, bf16[4096,128]{1,0:T(8,128)(2,1)} %v_weight.1, bf16[2048,4096]{1,0:T(8,128)(2,1)} %out_weight.1, bf16[2048,128]{1,0:T(8,128)(2,1)} %cache_keys.1, ...), custom_call_target="tpu_custom_call" | custom-call | tf_op jit(solution)/shard_map/pallas_call | solution.py:476
  58.1 1.6 %copy.11 = bf16[16,4096]{1,0:T(8,128)(2,1)} copy(bf16[16,4096]{1,0:T(8,128)(2,1)} %shard_map.91) | data formatting | bytes 262144

commit v2 on v1

--- a/solution.py
+++ b/solution.py
@@ -10,9 +10,10 @@
 
 BF = jnp.bfloat16
 F32 = jnp.float32
-WIRE = jnp.float32
-TILE = 256
+I16 = jnp.int16
+TILE = 1024
 ROWS = 16
+LEVELS = 32000.0
 
 
 def fused(
@@ -43,6 +44,9 @@
     wire,
     recv_end,
     recv_mid,
+    s_wire,
+    s_end,
+    s_mid,
     fresh,
     q_full,
     scores,
@@ -64,6 +68,8 @@
     tok_sem,
     up_sem,
     across_sem,
+    s_up_sem,
+    s_across_sem,
     down_sem,
     o_up_sem,
     o_across_sem,
@@ -182,10 +188,43 @@
         return pl.ds(c * gw, gw if c < groups else 2 * hd)
 
     def up(c):
-        return remote(wire.at[:, span_of(c)], recv_end.at[:, span_of(c)], up_sem.at[c], "gx", inner)
+        return (
+            remote(s_wire.at[c], s_end.at[c], s_up_sem.at[c], "gx", inner),
+            remote(wire.at[:, span_of(c)], recv_end.at[:, span_of(c)], up_sem.at[c], "gx", inner),
+        )
 
     def over(c):
-        return remote(wire.at[:, span_of(c)], recv_mid.at[:, span_of(c)], across_sem.at[c], "gx", other)
+        return (
+            remote(s_wire.at[c], s_mid.at[c], s_across_sem.at[c], "gx", other),
+            remote(
+                wire.at[:, span_of(c)], recv_mid.at[:, span_of(c)], across_sem.at[c], "gx", other
+            ),
+        )
+
+    def heads_of(c):
+        return hpg if c < groups else 2
+
+    def encode(c, y):
+        steps = []
+        for h in range(heads_of(c)):
+            z = y[:, h * hd : (h + 1) * hd]
+            top = jnp.max(jnp.abs(z), axis=1, keepdims=True)
+            top = jnp.where(top > 1e-30, top, 1.0)
+            code = jnp.round(z * (LEVELS / top)).astype(jnp.int32)
+            wire[:, pl.ds(c * gw + h * hd, hd)] = code.astype(I16)
+            steps.append(top * (1.0 / LEVELS))
+        s_wire[c] = to_lanes(steps)
+
+    def decode(c, ref, steps):
+        tile = steps[c]
+        return jnp.concatenate(
+            [
+                ref[:, pl.ds(c * gw + h * hd, hd)].astype(jnp.int32).astype(F32)
+                * from_lanes(tile, h)
+                for h in range(heads_of(c))
+            ],
+            axis=1,
+        )
 
     def down(c):
         return remote(q_full.at[:, span_of(c)], q_full.at[:, span_of(c)], down_sem.at[c], "gx", outer)
@@ -219,32 +258,30 @@
             wk_copy.wait()
             wv_copy.wait()
 
-        @pl.loop(0, span // TILE)
-        def _(i):
-            at = pl.multiple_of(i * TILE, TILE)
-            w = wq[:, pl.ds(base + at, TILE)] if c < groups else wkv[:, pl.ds(at, TILE)]
-            y = jnp.dot(
-                tok_full[...].reshape(total, -1), w, preferred_element_type=F32
-            )
-            part[:, pl.ds(base + at, TILE)] = y
-
-            @pl.when(end)
-            def _():
-                wire[:, pl.ds(base + at, TILE)] = y.astype(WIRE)
+        w = wq[:, pl.ds(base, span)] if c < groups else wkv[...]
+        y = jnp.dot(tok_full[...].reshape(total, -1), w, preferred_element_type=F32)
+
+        @pl.when(mid)
+        def _():
+            part[:, pl.ds(base, span)] = y
 
         @pl.when(end)
         def _():
-            up(c).start()
+            encode(c, y)
+            for copy in up(c):
+                copy.start()
 
     def pass_on(c):
         @pl.when(mid)
         def _():
-            up(c).wait_recv()
+            for copy in up(c):
+                copy.wait_recv()
             cols = span_of(c)
-            y = part[:, cols] + recv_end[:, cols].astype(F32)
+            y = part[:, cols] + decode(c, recv_end, s_end)
             part[:, cols] = y
-            wire[:, cols] = y.astype(WIRE)
-            over(c).start()
+            encode(c, y)
+            for copy in over(c):
+                copy.start()
 
     def settle(c):
         if c == groups:
@@ -253,9 +290,10 @@
 
         @pl.when(mid)
         def _():
-            over(c).wait_recv()
+            for copy in over(c):
+                copy.wait_recv()
             cols = span_of(c)
-            y = (part[:, cols] + recv_mid[:, cols].astype(F32)).astype(BF)
+            y = (part[:, cols] + decode(c, recv_mid, s_mid)).astype(BF)
             if c == groups:
                 fresh[...] = y.reshape(2, half, 2 * hd)
                 own = fresh[ix - 1]
@@ -420,7 +458,7 @@
     tok_relay.start()
     tok_pair.wait_recv()
     tok_relay.wait_recv()
-    steps = ('Pk', 'P0', 'P1', 'Xk', 'P2', 'X0', 'P3', 'X1', 'Yk', 'Y0', 'X2', 'Y1', 'X3', 'A0', 'Y2', 'A1', 'Y3', 'A2', 'A3', 'U0', 'U1', 'V0', 'U2', 'V1', 'M0', 'U3', 'V2', 'M1', 'V3', 'M2', 'M3')
+    steps = ('Pk', 'P0', 'P1', 'Xk', 'P2', 'X0', 'P3', 'X1', 'Yk', 'Y0', 'X2', 'Y1', 'X3', 'A0', 'Y2', 'A1', 'Y3', 'A2', 'A3', 'U0', 'U1', 'V0', 'U2', 'V1', 'U3', 'V2', 'M0', 'V3', 'M1', 'M2', 'M3')
     table = dict(P=project, X=pass_on, Y=settle, A=attend, U=merge, V=finish, M=mix)
     for step in steps:
         table[step[0]](groups if step[1] == "k" else int(step[1]))
@@ -441,7 +479,8 @@
     @pl.when(end)
     def _():
         for c in range(groups + 1):
-            up(c).wait_send()
+            for copy in up(c):
+                copy.wait_send()
         for c in range(groups):
             for copy in o_up(c):
                 copy.wait_send()
@@ -449,7 +488,8 @@
     @pl.when(mid)
     def _():
         for c in range(groups + 1):
-            over(c).wait_send()
+            for copy in over(c):
+                copy.wait_send()
         for c in range(groups):
             down(c).wait_send()
             o_down(c).wait_send()
@@ -488,9 +528,12 @@
             pltpu.VMEM((512, hd), BF),
             pltpu.VMEM((total, rows), F32),
             pltpu.VMEM((total, width + 2 * hd), F32),
-            pltpu.VMEM((total, width + 2 * hd), WIRE),
-            pltpu.VMEM((total, width + 2 * hd), WIRE),
-            pltpu.VMEM((total, width + 2 * hd), WIRE),
+            pltpu.VMEM((total, width + 2 * hd), I16),
+            pltpu.VMEM((total, width + 2 * hd), I16),
+            pltpu.VMEM((total, width + 2 * hd), I16),
+            pltpu.VMEM((chunks, 8, 128), F32),
+            pltpu.VMEM((chunks, 8, 128), F32),
+            pltpu.VMEM((chunks, 8, 128), F32),
             pltpu.VMEM((2, total // 2, 2 * hd), BF),
             pltpu.VMEM((total, width), BF),
             pltpu.VMEM((hpg * total, rows), F32),
@@ -510,6 +553,8 @@
             pltpu.VMEM((ROWS, out_cols), BF),
             dma((5 + 2 * groups,)),
             dma((3, 2)),
+            dma((chunks, 2)),
+            dma((chunks, 2)),
             dma((chunks, 2)),
             dma((chunks, 2)),
             dma((groups, 2)),

time: 59.8 us -> 50.1 us (0.84)
  Pallas kernels: 58.1 us -> 48.3 us
    pallas_call x1, Pallas kernels: 58.1 us -> 48.3 us  [fused_body(): pl.pallas_call(functools.partial(fused, nx, ny, heads, hd, hpg), out_shap...]
where the time goes in v2:
time: 50.1 us; the launch traced here: 49.9 us
  Pallas kernels  48.3 us (96%)
  local copies, waits for them, and re-layouts  1.57 us (3%)
    pallas_call x1, Pallas kernels, fused_body(): pl.pallas_call(functools.partial(fused, nx, ny, heads, hd, hpg), out_shap...  48.3 us
    unnamed x1, local copies, waits for them, and re-layouts  1.57 us

profile of v2, /device:TPU:0, one launch (start us, length us, event | category | flops | bytes accessed | tf_op | source)
XLA Modules:
  0.0 49.9 jit_solution(17027086254047979636)
XLA Ops:
  0.0 48.3 %shard_map.91 = bf16[16,4096]{1,0:T(8,128)(2,1)} custom-call(bf16[16,4096]{1,0:T(8,128)(2,1)} %tokens.1, bf16[4096,2048]{1,0:T(8,128)(2,1)} %q_weight.1, bf16[4096,128]{1,0:T(8,128)(2,1)} %k_weight.1, bf16[4096,128]{1,0:T(8,128)(2,1)} %v_weight.1, bf16[2048,4096]{1,0:T(8,128)(2,1)} %out_weight.1, bf16[2048,128]{1,0:T(8,128)(2,1)} %cache_keys.1, ...), custom_call_target="tpu_custom_call" | custom-call | tf_op jit(solution)/shard_map/pallas_call | solution.py:516
  48.3 1.6 %copy.11 = bf16[16,4096]{1,0:T(8,128)(2,1)} copy(bf16[16,4096]{1,0:T(8,128)(2,1)} %shard_map.91) | data formatting | bytes 262144

commit v3 on v2

--- a/solution.py
+++ b/solution.py
@@ -143,9 +143,15 @@
         signal("gx", other)
         pl.semaphore_wait(barrier, 4)
 
-    tok_across = remote(tokens, tok_full.at[iy], tok_sem.at[0], "gy", across)
-    tok_across.start()
-    tok_pair = remote(tokens, tok_full.at[iy], tok_sem.at[1], "gy", sibling)
+    half_depth = tokens.shape[1] // 2
+    halves = [pl.ds(0, half_depth), pl.ds(half_depth, half_depth)]
+    tok_across = [
+        remote(tokens.at[:, f], tok_full.at[iy, :, f], tok_sem.at[i], "gy", across)
+        for i, f in enumerate(halves)
+    ]
+    for copy in tok_across:
+        copy.start()
+    tok_pair = remote(tokens, tok_full.at[iy], tok_sem.at[4], "gy", sibling)
     tok_pair.start()
 
     tid_row = tenants[...].astype(F32)
@@ -453,12 +459,16 @@
         pair(spans - 1)
 
     own_tokens.wait()
-    tok_across.wait_recv()
-    tok_relay = remote(tok_full.at[across], tok_full.at[across], tok_sem.at[2], "gy", sibling)
-    tok_relay.start()
+    tok_relay = []
+    for i, f in enumerate(halves):
+        tok_across[i].wait_recv()
+        block = tok_full.at[across, :, f]
+        tok_relay.append(remote(block, block, tok_sem.at[2 + i], "gy", sibling))
+        tok_relay[i].start()
     tok_pair.wait_recv()
-    tok_relay.wait_recv()
-    steps = ('Pk', 'P0', 'P1', 'Xk', 'P2', 'X0', 'P3', 'X1', 'Yk', 'Y0', 'X2', 'Y1', 'X3', 'A0', 'Y2', 'A1', 'Y3', 'A2', 'A3', 'U0', 'U1', 'V0', 'U2', 'V1', 'U3', 'V2', 'M0', 'V3', 'M1', 'M2', 'M3')
+    for copy in tok_relay:
+        copy.wait_recv()
+    steps = ('Pk', 'P0', 'P1', 'Xk', 'P2', 'X0', 'P3', 'X1', 'Yk', 'Y0', 'X2', 'Y1', 'X3', 'A0', 'Y2', 'A1', 'Y3', 'A2', 'A3', 'U0', 'U1', 'V0', 'U2', 'V1', 'U3', 'V2', 'V3', 'M0', 'M1', 'M2', 'M3')
     table = dict(P=project, X=pass_on, Y=settle, A=attend, U=merge, V=finish, M=mix)
     for step in steps:
         table[step[0]](groups if step[1] == "k" else int(step[1]))
@@ -469,9 +479,9 @@
         cell_copy(n).wait_recv()
         out[:, cols] = (y + recv4[:, cols].astype(F32)).astype(BF)
 
-    tok_across.wait_send()
     tok_pair.wait_send()
-    tok_relay.wait_send()
+    for copy in tok_across + tok_relay:
+        copy.wait_send()
     for n in range(spans):
         pair_copy(n).wait_send()
         cell_copy(n).wait_send()
@@ -552,7 +562,7 @@
             pltpu.VMEM((ROWS, out_cols), BF),
             pltpu.VMEM((ROWS, out_cols), BF),
             dma((5 + 2 * groups,)),
-            dma((3, 2)),
+            dma((5, 2)),
             dma((chunks, 2)),
             dma((chunks, 2)),
             dma((chunks, 2)),

time: 50.1 us -> 49.9 us (level)
  no operation moved by 1% of the time
where the time goes in v3:
time: 49.9 us; the launch traced here: 49.7 us
  Pallas kernels  48.1 us (96%)
  local copies, waits for them, and re-layouts  1.57 us (3%)
    pallas_call x1, Pallas kernels, fused_body(): pl.pallas_call(functools.partial(fused, nx, ny, heads, hd, hpg), out_shap...  48.1 us
    unnamed x1, local copies, waits for them, and re-layouts  1.57 us

profile of v3, /device:TPU:0, one launch (start us, length us, event | category | flops | bytes accessed | tf_op | source)
XLA Modules:
  0.0 49.7 jit_solution(15003944744283912540)
XLA Ops:
  0.0 48.1 %shard_map.91 = bf16[16,4096]{1,0:T(8,128)(2,1)} custom-call(bf16[16,4096]{1,0:T(8,128)(2,1)} %tokens.1, bf16[4096,2048]{1,0:T(8,128)(2,1)} %q_weight.1, bf16[4096,128]{1,0:T(8,128)(2,1)} %k_weight.1, bf16[4096,128]{1,0:T(8,128)(2,1)} %v_weight.1, bf16[2048,4096]{1,0:T(8,128)(2,1)} %out_weight.1, bf16[2048,128]{1,0:T(8,128)(2,1)} %cache_keys.1, ...), custom_call_target="tpu_custom_call" | custom-call | tf_op jit(solution)/shard_map/pallas_call | solution.py:526
  48.2 1.6 %copy.11 = bf16[16,4096]{1,0:T(8,128)(2,1)} copy(bf16[16,4096]{1,0:T(8,128)(2,1)} %shard_map.91) | data formatting | bytes 262144
